TPU v7x, 32 devices: a whole 2x2x4 slice. The times are simulated.
32 devices in a mesh: lblk: 16 (over z, x, core), tile: 2 (over y).
Axes of the slice: x: 2, y: 2, z: 4, core: 2. Of those that a mesh axis runs over, the one named last changes fastest.
Arguments:
- wavefunction: float32 [2048, 2, 16, 128], P('lblk', None, 'tile'), may hold values from -6 to 6
- l_table: int32 [2048, 2], P('lblk'), may hold values from 0 to 15
- coupling: float32 [16, 8, 128, 128], P('lblk'), may hold values from -2 to 2
- selection: int32 [16, 8], P('lblk'), may hold values 0 or 1
- dipole: float32 [16, 2, 128, 128], P('lblk'), may hold values from -0.5 to 0.5
- field: float32 [1], replicated, may hold values from -0.1 to 0.1
Outputs:
- propagated: float32 [2048, 2, 16, 128], P('lblk', None, 'tile')
All inputs are finite; a program needn't handle non-finite values. No bound on the sum of `selection` on one device may be relied on, other than what follows from the above.
Results may differ from a plain program's by a relative error of at most 0.0001.
Values sent between devices are 32-bit elements; how exact they have to be, the bound alone decides.
A program may use at most 64 MiB of HBM per device.

v0:
```python
import functools

import jax
import jax.numpy as jnp
from jax import lax
from jax.experimental import pallas as pl
from jax.experimental.pallas import tpu as pltpu
from jax.sharding import PartitionSpec as P

TAYLOR = 4
time_step = 0.03
grid_step = 0.5
radius_start = 8.0
F32 = jnp.float32
BF16 = jnp.bfloat16
MESH = pl.DeviceIdType.MESH
HALO = 2
ROWS = 2


def halves(value):
    high = value.astype(BF16)
    return high, (value - high.astype(F32)).astype(BF16)


def three_pass(value_list):
    pairs = [halves(value) for value in value_list]
    high = [pair[0] for pair in pairs]
    return jnp.concatenate(high + high + [pair[1] for pair in pairs], axis=0)


def kernel(
    blocks, tiles, cols, wave, angular, coupling, dipole, selection, field, out,
    state, near, weights, lower, w_stack, d_stack, part, totals, from_pair,
    psi_sem, wgt_sem, core_sem, z_sem, down_sem, up_sem, dcore_sem, dz_sem, back_sem,
):
    ch = coupling.shape[1]
    nmp = coupling.shape[0]
    quad = nmp // 2
    width = wave.shape[2]
    rows = width // cols
    edge = HALO * cols
    mid = pl.ds(edge, width)

    me = lax.axis_index("lblk")
    tile = lax.axis_index("tile")
    core = me % 2
    pair = (me // 2) % 2
    other = 1 - pair
    quad_at = me // 4
    last_quad = blocks // 4 - 1
    to_pair = {"lblk": me + 2 - 4 * pair}
    to_core = {"lblk": me + 1 - 2 * core}
    to_z = {"lblk": me + 6 * core - 3}
    to_low = {"tile": tile - 1}
    to_high = {"tile": tile + 1}
    has_z = jnp.logical_or(
        jnp.logical_and(core == 1, quad_at < last_quad), jnp.logical_and(core == 0, quad_at > 0)
    )
    has_low = tile > 0
    has_high = tile < tiles - 1

    def remote(src, dst, sems, target):
        return pltpu.make_async_remote_copy(
            src_ref=src, dst_ref=dst, send_sem=sems.at[0], recv_sem=sems.at[1],
            device_id=target, device_id_type=MESH,
        )

    def psi_copy():
        return remote(wave.at[other], state.at[0, pair, :, mid], psi_sem, to_pair)

    def weight_copy():
        return remote(weights.at[pair], weights.at[pair], wgt_sem, to_pair)

    def core_copy(step, b):
        return remote(state.at[step, b, :, mid], near.at[step, core + b], core_sem.at[step, b], to_core)

    def z_copy(step):
        return remote(state.at[step, core, :, mid], near.at[step, 2 * (1 - core)], z_sem.at[step], to_z)

    def low_copy(step, b):
        return remote(
            state.at[step, b, :, pl.ds(edge, edge)], state.at[step, b, :, pl.ds(edge + width, edge)],
            down_sem.at[step, b], to_low,
        )

    def high_copy(step, b):
        return remote(
            state.at[step, b, :, pl.ds(width, edge)], state.at[step, b, :, pl.ds(0, edge)],
            up_sem.at[step, b], to_high,
        )

    def send_block(step, b):
        @pl.when(jnp.logical_and(b == core, has_z))
        def _():
            z_copy(step).start()

        @pl.when(has_low)
        def _():
            low_copy(step, b).start()

        @pl.when(has_high)
        def _():
            high_copy(step, b).start()

        core_copy(step, b).start()

    def wait_sent(step, b):
        @pl.when(jnp.logical_and(b == core, has_z))
        def _():
            z_copy(step).wait_send()

        @pl.when(has_low)
        def _():
            low_copy(step, b).wait_send()

        @pl.when(has_high)
        def _():
            high_copy(step, b).wait_send()

        core_copy(step, b).wait_send()

    def wait_halo(step, b):
        @pl.when(has_high)
        def _():
            low_copy(step, b).wait_recv()

        @pl.when(has_low)
        def _():
            high_copy(step, b).wait_recv()

    def back_copy(which):
        return remote(totals.at[which, other], from_pair.at[which], back_sem.at[which], to_pair)

    def dcore_low(b):
        return remote(weights.at[b, pl.ds(nmp, 2)], lower.at[b], dcore_sem.at[b], to_core)

    def dcore_high():
        return remote(weights.at[0, pl.ds(nmp, 2)], lower.at[1], dcore_sem.at[1], to_core)

    def dz_copy():
        return remote(weights.at[1, pl.ds(nmp, 2)], lower.at[0], dz_sem, to_z)

    barrier = pltpu.get_barrier_semaphore()
    for target, there in (
        (to_pair, None), (to_core, None), (to_z, has_z), (to_low, has_low), (to_high, has_high),
    ):
        if there is None:
            pl.semaphore_signal(barrier, inc=1, device_id=target, device_id_type=MESH)
        else:
            @pl.when(there)
            def _(target=target):
                pl.semaphore_signal(barrier, inc=1, device_id=target, device_id_type=MESH)
    state[0, pair, :, mid] = wave[pair]
    peers = 2
    for there in (has_z, has_low, has_high):
        peers = peers + there.astype(jnp.int32)
    pl.semaphore_wait(barrier, peers)

    psi_copy().start()
    send_block(0, pair)

    for k in range(nmp):
        weights[pair, k] = (0.5 * selection[0, k].astype(F32)) * (coupling[k] + coupling[k].T)
    weights[pair, nmp] = dipole[0]
    weights[pair, nmp + 1] = dipole[1]
    lane = lax.broadcasted_iota(jnp.int32, (ch, ch), 1)
    momenta = angular[...].astype(F32)
    momenta = 0.5 * momenta * (momenta + 1.0)
    weights[pair, nmp + 2] = jnp.where(lane < ch // 2, momenta[:, 0:1], momenta[:, 1:2])
    weight_copy().start()

    for step in range(TAYLOR):
        for b in range(2):
            @pl.when(jnp.logical_not(has_low))
            def _(step=step, b=b):
                state[step, b, :, pl.ds(0, edge)] = jnp.zeros((ch, edge), F32)

            @pl.when(jnp.logical_not(has_high))
            def _(step=step, b=b):
                state[step, b, :, pl.ds(edge + width, edge)] = jnp.zeros((ch, edge), F32)

        @pl.when(jnp.logical_not(has_z))
        def _(step=step):
            near[step, 2 * core] = jnp.zeros((ch, width), F32)

    @pl.when(jnp.logical_and(core == 0, jnp.logical_not(has_z)))
    def _():
        lower[0] = jnp.zeros((2, ch, ch), F32)

    def stack_weights(b):
        for a in range(quad):
            at = pl.ds(a * ch, ch)
            for part_at, k in ((0, a), (1, a + quad)):
                high, low = halves(weights[b, k])
                w_stack[b, at, pl.ds(part_at * ch, ch)] = high
                w_stack[b, at, pl.ds((2 + part_at) * ch, ch)] = low
                w_stack[b, at, pl.ds((4 + part_at) * ch, ch)] = high

    def stack_dipoles(b):
        for a in range(2):
            at = pl.ds(a * ch, ch)
            for part_at, matrix in ((0, weights[b, nmp + a]), (1, lower[b, a].T)):
                high, low = halves(matrix)
                d_stack[b, at, pl.ds(part_at * ch, ch)] = high
                d_stack[b, at, pl.ds((2 + part_at) * ch, ch)] = low
                d_stack[b, at, pl.ds((4 + part_at) * ch, ch)] = high

    span = ROWS * cols

    def radii(at):
        index = lax.broadcasted_iota(jnp.int32, (1, span), 1)
        row = tile * rows + at * ROWS + index // cols
        one = radius_start + grid_step * row.astype(F32)
        two = radius_start + grid_step * (index % cols).astype(F32)
        return one, two

    def multipoles(step, b):
        def body(at, carry):
            one, two = radii(at)
            larger = jnp.maximum(one, two)
            ratio = jnp.minimum(one, two) / larger
            power = ratio
            for _ in range(quad - 1):
                power = power * ratio
            value = state[step, b, :, pl.ds(pl.multiple_of(edge + at * span, cols), span)]
            stacked = three_pass([value, power * value])
            product = jnp.dot(w_stack[b], stacked, preferred_element_type=F32)
            result = product[(quad - 1) * ch:]
            for a in range(quad - 2, -1, -1):
                result = product[a * ch:(a + 1) * ch] + ratio * result
            part[b, :, pl.ds(pl.multiple_of(at * span, cols), span)] = result / larger
            return carry

        lax.fori_loop(0, rows // ROWS, body, 0)

    def finish(step, b, scale):
        strength = field[0]
        c_one = weights[b, nmp + 2, :, 0:1]
        c_two = weights[b, nmp + 2, :, ch // 2:ch // 2 + 1]
        lane_at = lax.broadcasted_iota(jnp.int32, (1, cols), 1)

        def body(at, carry):
            one, two = radii(at)
            here = pl.ds(pl.multiple_of(at * span, cols), span)
            up = near[step, b + 1, :, here]
            down = near[step, b, :, here]
            product = jnp.dot(d_stack[b], three_pass([up, down]), preferred_element_type=F32)
            dipole_term = (strength * one) * product[:ch] + (strength * two) * product[ch:]

            def window(offset):
                start = pl.multiple_of(at * span + (HALO + offset) * cols, cols)
                return state[step, b, :, pl.ds(start, span)]

            value = window(0)
            around = 16.0 * (window(-1) + window(1)) - (window(-2) + window(2))
            pieces = []
            for r in range(ROWS):
                line = value[:, r * cols:(r + 1) * cols]

                def moved(by):
                    rolled = pltpu.roll(line, by % cols, 1)
                    inside = lane_at >= by if by > 0 else lane_at < cols + by
                    return jnp.where(inside, rolled, 0.0)

                pieces.append(16.0 * (moved(1) + moved(-1)) - (moved(2) + moved(-2)))
            around = around + jnp.concatenate(pieces, axis=1)
            factor = -0.5 / (12.0 * grid_step * grid_step)
            centre = (
                (-60.0 * factor) - 2.0 / one - 2.0 / two + c_one / (one * one) + c_two / (two * two)
            )
            applied = factor * around + centre * value + part[b, :, here] + dipole_term
            term = scale * applied
            start = pl.multiple_of(edge + at * span, cols)
            state[step + 1, b, :, pl.ds(start, span)] = term
            which = (step + 1) % 2
            totals[which, b, :, here] = totals[which, b, :, here] + term
            return carry

        lax.fori_loop(0, rows // ROWS, body, 0)

    stack_weights(pair)
    multipoles(0, pair)
    psi_copy().wait_recv()
    send_block(0, other)
    for b in range(2):
        totals[0, b] = state[0, b, :, mid]
        totals[1, b] = jnp.zeros((ch, width), F32)
    weight_copy().wait_recv()

    @pl.when(core == 0)
    def _():
        dcore_low(0).start()
        dcore_low(1).start()

    @pl.when(core == 1)
    def _():
        dcore_high().start()

        @pl.when(has_z)
        def _():
            dz_copy().start()

    stack_weights(other)
    multipoles(0, other)

    @pl.when(core == 1)
    def _():
        dcore_low(0).wait_recv()
        dcore_low(1).wait_recv()

    @pl.when(core == 0)
    def _():
        dcore_high().wait_recv()

        @pl.when(has_z)
        def _():
            dz_copy().wait_recv()

    stack_dipoles(0)
    stack_dipoles(1)

    def order(step, carry):
        @pl.when(step > 0)
        def _():
            multipoles(step, other)
            multipoles(step, pair)

        sign = ((2 * ((step + 1) % 2) - 1) * (2 * pair - 1)).astype(F32)
        scale = sign * (time_step / (step + 1).astype(F32))
        core_copy(step, 0).wait_recv()
        core_copy(step, 1).wait_recv()

        @pl.when(has_z)
        def _():
            z_copy(step).wait_recv()

        for b in (other, pair):
            wait_halo(step, b)
            finish(step, b, scale)

            @pl.when(step < TAYLOR - 1)
            def _():
                send_block(step + 1, b)

            if b is other:
                @pl.when(step >= TAYLOR - 2)
                def _():
                    back_copy((step + 1) % 2).start()
        return carry

    lax.fori_loop(0, TAYLOR, order, 0)

    back_copy(1).wait_recv()
    back_copy(0).wait_recv()
    out[pair] = totals[0, pair] + from_pair[1]
    out[other] = totals[1, pair] + from_pair[0]

    psi_copy().wait_send()
    weight_copy().wait_send()
    for step in range(TAYLOR):
        for b in range(2):
            wait_sent(step, b)

    @pl.when(core == 0)
    def _():
        dcore_low(0).wait_send()
        dcore_low(1).wait_send()

    @pl.when(core == 1)
    def _():
        dcore_high().wait_send()

        @pl.when(has_z)
        def _():
            dz_copy().wait_send()

    back_copy(0).wait_send()
    back_copy(1).wait_send()


def per_device(blocks, tiles, wavefunction, l_table, coupling, selection, dipole, field):
    ch, parts, rows, cols = wavefunction.shape
    width = rows * cols
    nmp = coupling.shape[1]
    edge = HALO * cols
    wave = jnp.transpose(wavefunction, (1, 0, 2, 3)).reshape(parts, ch, width)
    vmem = pl.BlockSpec(memory_space=pltpu.VMEM)
    smem = pl.BlockSpec(memory_space=pltpu.SMEM)
    dma = pltpu.SemaphoreType.DMA
    result = pl.pallas_call(
        functools.partial(kernel, blocks, tiles, cols),
        out_shape=jax.ShapeDtypeStruct((parts, ch, width), F32),
        in_specs=[vmem, vmem, vmem, vmem, smem, smem],
        out_specs=vmem,
        scratch_shapes=[
            pltpu.VMEM((TAYLOR + 1, 2, ch, width + 2 * edge), F32),
            pltpu.VMEM((TAYLOR, 3, ch, width), F32),
            pltpu.VMEM((2, nmp + 3, ch, ch), F32),
            pltpu.VMEM((2, 2, ch, ch), F32),
            pltpu.VMEM((2, nmp // 2 * ch, 6 * ch), BF16),
            pltpu.VMEM((2, 2 * ch, 6 * ch), BF16),
            pltpu.VMEM((2, ch, width), F32),
            pltpu.VMEM((2, 2, ch, width), F32),
            pltpu.VMEM((2, ch, width), F32),
            dma((2,)),
            dma((2,)),
            dma((TAYLOR, 2, 2)),
            dma((TAYLOR, 2)),
            dma((TAYLOR, 2, 2)),
            dma((TAYLOR, 2, 2)),
            dma((2, 2)),
            dma((2,)),
            dma((2, 2)),
        ],
        compiler_params=pltpu.CompilerParams(
            collective_id=0, has_side_effects=True, vmem_limit_bytes=48 * 1024 * 1024
        ),
    )(wave, l_table, coupling[0], dipole[0], selection, field)
    return jnp.transpose(result.reshape(parts, ch, rows, cols), (1, 0, 2, 3))


def solution(mesh):
    placed = (
        P("lblk", None, "tile", None),
        P("lblk", None),
        P("lblk", None, None, None),
        P("lblk", None),
        P("lblk", None, None, None),
        P(),
    )
    return jax.shard_map(
        functools.partial(per_device, mesh.shape["lblk"], mesh.shape["tile"]),
        mesh=mesh,
        in_specs=placed,
        out_specs=P("lblk", None, "tile", None),
        check_vma=False,
    )
```

profile of v0, /device:TPU:13, one launch (start us, length us, event | category | flops | bytes accessed | tf_op | source)
XLA Modules:
  0.0 84.7 jit_solution(16574434078024158148)
XLA Ops:
  0.7 0.0 copy-start.3
  0.7 0.7 copy-done.3
  1.3 0.1 copy.8.angular
  1.4 1.7 %reshape.8 = f32[2,128,1024]{2,0,1:T(2,128)S(1)} reshape(f32[2,128,8,128]{3,2,0,1:T(8,128)} %bitcast.21) | data formatting | bytes 2097152 | tf_op jit(solution)/shard_map/reshape | solution.py:387
  3.2 0.0 copy-start
  3.2 0.0 copy-start.1
  3.2 0.0 copy-start.2
  3.2 0.3 copy.10.wave
  3.6 0.7 copy-done
  4.2 0.0 copy-done.1
  4.3 0.0 copy-done.2
  4.3 79.2 %shard_map.64 = f32[2,128,1024]{2,1,0:T(8,128)S(1)} custom-call(f32[2,128,1024]{2,1,0:T(8,128)S(1)} %copy.10.wave, s32[128,2]{1,0:T(8,128)S(1)} %copy.8.angular, f32[8,128,128]{2,1,0:T(8,128)S(1)} %bitcast.18, f32[2,128,128]{2,1,0:T(8,128)S(1)} %bitcast.19, s32[1,8]{1,0:T(1,128)S(1)} %copy-done.2, f32[1]{0:T(128)S(6)} %copy.13.field), custom_call_target="tpu_custom_call" | custom-call | tf_op jit(solution)/shard_map/pallas_call | solution.py:391
  83.4 0.2 copy.11
  83.7 1.1 %copy_bitcast_fusion = f32[128,2,8,128]{3,2,1,0:T(8,128)} fusion(f32[2,128,8,128]{3,2,1,0:T(8,128)S(1)} %bitcast.20), kind=kLoop, calls=%fused_computation | loop fusion | bytes 2097152 | tf_op jit(solution)/shard_map/transpose | solution.py:420
Async XLA Ops:
  0.7 0.7 copy-start.3
  3.2 1.0 %copy-start = (f32[1,8,128,128]{3,2,1,0:T(8,128)S(1)}, f32[1,8,128,128]{3,2,1,0:T(8,128)}, u32[]{:S(2)}) copy-start(f32[1,8,128,128]{3,2,1,0:T(8,128)} %param.8) | copy-start | bytes 1572868
  3.2 1.1 %copy-start.1 = (f32[1,2,128,128]{3,2,1,0:T(8,128)S(1)}, f32[1,2,128,128]{3,2,1,0:T(8,128)}, u32[]{:S(2)}) copy-start(f32[1,2,128,128]{3,2,1,0:T(8,128)} %param.10) | copy-start | bytes 393220
  3.2 1.0 %copy-start.2 = (s32[1,8]{1,0:T(1,128)S(1)}, s32[1,8]{1,0:T(1,128)}, u32[]{:S(2)}) copy-start(s32[1,8]{1,0:T(1,128)} %selection.1) | copy-start | bytes 100
where the time goes:
time: 85 us; the launch traced here: 84.7 us
  Pallas kernels  79.2 us (93%)
  local copies, waits for them, and re-layouts  4.81 us (6%)
    pallas_call x1, Pallas kernels, per_device(): pl.pallas_call(functools.partial(kernel, blocks, tiles, cols), out_shape=...  79.2 us
    reshape x2, local copies, waits for them, and re-layouts, per_device(): wave = jnp.transpose(wavefunction, (1, 0, 2, 3)).reshape(parts, ch, width)  2.08 us

commit v1 on v0

--- a/solution.py
+++ b/solution.py
@@ -30,15 +30,18 @@
 
 
 def kernel(
-    blocks, tiles, cols, wave, angular, coupling, dipole, selection, field, out,
-    state, near, weights, lower, w_stack, d_stack, part, totals, from_pair,
-    psi_sem, wgt_sem, core_sem, z_sem, down_sem, up_sem, dcore_sem, dz_sem, back_sem,
+    blocks, tiles, rows, wave_in, angular, coupling_in, dipole_in, selection, field, out,
+    wave, coupling, dipole, start_other,
+    state, near, weights, central, lower, w_stack, d_stack, part, totals, from_pair,
+    load_sem, psi_sem, wgt_sem, core_sem, z_sem, down_sem, up_sem, dcore_sem, dz_sem, back_sem,
 ):
     ch = coupling.shape[1]
     nmp = coupling.shape[0]
     quad = nmp // 2
-    width = wave.shape[2]
-    rows = width // cols
+    cols = wave.shape[1]
+    width = rows * cols
+    stride = 2 * rows
+    side = (quad + 2) * ch
     edge = HALO * cols
     mid = pl.ds(edge, width)
 
@@ -67,7 +70,7 @@
         )
 
     def psi_copy():
-        return remote(wave.at[other], state.at[0, pair, :, mid], psi_sem, to_pair)
+        return remote(start_other, state.at[0, pair, :, mid], psi_sem, to_pair)
 
     def weight_copy():
         return remote(weights.at[pair], weights.at[pair], wgt_sem, to_pair)
@@ -133,13 +136,20 @@
         return remote(totals.at[which, other], from_pair.at[which], back_sem.at[which], to_pair)
 
     def dcore_low(b):
-        return remote(weights.at[b, pl.ds(nmp, 2)], lower.at[b], dcore_sem.at[b], to_core)
+        return remote(weights.at[b, pl.ds(quad * ch, 2 * ch)], lower.at[b], dcore_sem.at[b], to_core)
 
     def dcore_high():
-        return remote(weights.at[0, pl.ds(nmp, 2)], lower.at[1], dcore_sem.at[1], to_core)
+        return remote(weights.at[0, pl.ds(quad * ch, 2 * ch)], lower.at[1], dcore_sem.at[1], to_core)
 
     def dz_copy():
-        return remote(weights.at[1, pl.ds(nmp, 2)], lower.at[0], dz_sem, to_z)
+        return remote(weights.at[1, pl.ds(quad * ch, 2 * ch)], lower.at[0], dz_sem, to_z)
+
+    loads = [
+        pltpu.make_async_copy(src, dst, load_sem.at[at])
+        for at, (src, dst) in enumerate(((wave_in, wave), (coupling_in, coupling), (dipole_in, dipole)))
+    ]
+    for load in loads:
+        load.start()
 
     barrier = pltpu.get_barrier_semaphore()
     for target, there in (
@@ -151,7 +161,13 @@
             @pl.when(there)
             def _(target=target):
                 pl.semaphore_signal(barrier, inc=1, device_id=target, device_id_type=MESH)
-    state[0, pair, :, mid] = wave[pair]
+    loads[0].wait()
+    for row in range(rows):
+        here = pl.ds(row * cols, cols)
+        start_other[:, here] = wave[pl.ds(other * rows + row, ch, stride=stride), :]
+        state[0, pair, :, pl.ds(edge + row * cols, cols)] = wave[
+            pl.ds(pair * rows + row, ch, stride=stride), :
+        ]
     peers = 2
     for there in (has_z, has_low, has_high):
         peers = peers + there.astype(jnp.int32)
@@ -160,15 +176,48 @@
     psi_copy().start()
     send_block(0, pair)
 
-    for k in range(nmp):
-        weights[pair, k] = (0.5 * selection[0, k].astype(F32)) * (coupling[k] + coupling[k].T)
-    weights[pair, nmp] = dipole[0]
-    weights[pair, nmp + 1] = dipole[1]
-    lane = lax.broadcasted_iota(jnp.int32, (ch, ch), 1)
+    def put_weight(b, k, matrix):
+        at = pl.ds(k % quad * ch, ch)
+        place = k // quad
+        high, low = halves(matrix)
+        w_stack[b, at, pl.ds(place * ch, ch)] = high
+        w_stack[b, at, pl.ds((2 + place) * ch, ch)] = low
+        w_stack[b, at, pl.ds((4 + place) * ch, ch)] = high
+
+    at_row = lax.broadcasted_iota(jnp.int32, (ch, ch), 0)
+    at_col = lax.broadcasted_iota(jnp.int32, (ch, ch), 1)
     momenta = angular[...].astype(F32)
     momenta = 0.5 * momenta * (momenta + 1.0)
-    weights[pair, nmp + 2] = jnp.where(lane < ch // 2, momenta[:, 0:1], momenta[:, 1:2])
+    weights[pair, pl.ds(side, 2)] = momenta
+    loads[1].wait()
+    loads[2].wait()
+    for k in range(quad):
+        both = []
+        for index in (k, k + quad):
+            matrix = (0.5 * selection[0, index].astype(F32)) * (coupling[index] + coupling[index].T)
+            weights[pair, pl.ds(side + 2 + index, 1)] = jnp.sum(
+                jnp.where(at_row == at_col, matrix, 0.0), axis=0, keepdims=True
+            )
+            both.append(matrix)
+        weights[pair, pl.ds(k * ch, ch)] = jnp.where(at_row < at_col, both[0], both[1])
+        put_weight(pair, k, both[0])
+        put_weight(pair, k + quad, both[1])
+    for a in range(2):
+        weights[pair, pl.ds((quad + a) * ch, ch)] = dipole[a]
     weight_copy().start()
+
+    def unpack(b):
+        for k in range(quad):
+            packed = weights[b, pl.ds(k * ch, ch)]
+            for index, keep in ((k, at_row < at_col), (k + quad, at_row > at_col)):
+                kept = jnp.where(keep, packed, 0.0)
+                diagonal = weights[b, pl.ds(side + 2 + index, 1)]
+                put_weight(b, index, jnp.where(at_row == at_col, diagonal, kept + kept.T))
+
+    def spread(b):
+        for a in range(2):
+            vector = weights[b, pl.ds(side + a, 1)]
+            central[b, a] = jnp.broadcast_to(vector, (cols, ch)).T
 
     for step in range(TAYLOR):
         for b in range(2):
@@ -186,21 +235,12 @@
 
     @pl.when(jnp.logical_and(core == 0, jnp.logical_not(has_z)))
     def _():
-        lower[0] = jnp.zeros((2, ch, ch), F32)
-
-    def stack_weights(b):
-        for a in range(quad):
-            at = pl.ds(a * ch, ch)
-            for part_at, k in ((0, a), (1, a + quad)):
-                high, low = halves(weights[b, k])
-                w_stack[b, at, pl.ds(part_at * ch, ch)] = high
-                w_stack[b, at, pl.ds((2 + part_at) * ch, ch)] = low
-                w_stack[b, at, pl.ds((4 + part_at) * ch, ch)] = high
+        lower[0] = jnp.zeros((2 * ch, ch), F32)
 
     def stack_dipoles(b):
         for a in range(2):
             at = pl.ds(a * ch, ch)
-            for part_at, matrix in ((0, weights[b, nmp + a]), (1, lower[b, a].T)):
+            for part_at, matrix in ((0, weights[b, pl.ds((quad + a) * ch, ch)]), (1, lower[b, pl.ds(a * ch, ch)].T)):
                 high, low = halves(matrix)
                 d_stack[b, at, pl.ds(part_at * ch, ch)] = high
                 d_stack[b, at, pl.ds((2 + part_at) * ch, ch)] = low
@@ -218,8 +258,8 @@
     def multipoles(step, b):
         def body(at, carry):
             one, two = radii(at)
-            larger = jnp.maximum(one, two)
-            ratio = jnp.minimum(one, two) / larger
+            inverse = 1.0 / jnp.maximum(one, two)
+            ratio = jnp.minimum(one, two) * inverse
             power = ratio
             for _ in range(quad - 1):
                 power = power * ratio
@@ -229,15 +269,13 @@
             result = product[(quad - 1) * ch:]
             for a in range(quad - 2, -1, -1):
                 result = product[a * ch:(a + 1) * ch] + ratio * result
-            part[b, :, pl.ds(pl.multiple_of(at * span, cols), span)] = result / larger
+            part[b, :, pl.ds(pl.multiple_of(at * span, cols), span)] = result * inverse
             return carry
 
         lax.fori_loop(0, rows // ROWS, body, 0)
 
     def finish(step, b, scale):
         strength = field[0]
-        c_one = weights[b, nmp + 2, :, 0:1]
-        c_two = weights[b, nmp + 2, :, ch // 2:ch // 2 + 1]
         lane_at = lax.broadcasted_iota(jnp.int32, (1, cols), 1)
 
         def body(at, carry):
@@ -266,8 +304,13 @@
                 pieces.append(16.0 * (moved(1) + moved(-1)) - (moved(2) + moved(-2)))
             around = around + jnp.concatenate(pieces, axis=1)
             factor = -0.5 / (12.0 * grid_step * grid_step)
+            inv_one, inv_two = 1.0 / one, 1.0 / two
+            c_one = jnp.concatenate([central[b, 0]] * ROWS, axis=1)
+            c_two = jnp.concatenate([central[b, 1]] * ROWS, axis=1)
             centre = (
-                (-60.0 * factor) - 2.0 / one - 2.0 / two + c_one / (one * one) + c_two / (two * two)
+                (-60.0 * factor - 2.0 * inv_one - 2.0 * inv_two)
+                + c_one * (inv_one * inv_one)
+                + c_two * (inv_two * inv_two)
             )
             applied = factor * around + centre * value + part[b, :, here] + dipole_term
             term = scale * applied
@@ -279,7 +322,7 @@
 
         lax.fori_loop(0, rows // ROWS, body, 0)
 
-    stack_weights(pair)
+    spread(pair)
     multipoles(0, pair)
     psi_copy().wait_recv()
     send_block(0, other)
@@ -301,7 +344,8 @@
         def _():
             dz_copy().start()
 
-    stack_weights(other)
+    unpack(other)
+    spread(other)
     multipoles(0, other)
 
     @pl.when(core == 1)
@@ -324,6 +368,9 @@
         @pl.when(step > 0)
         def _():
             multipoles(step, other)
+
+        @pl.when(jnp.logical_and(step > 0, step < TAYLOR - 1))
+        def _():
             multipoles(step, pair)
 
         sign = ((2 * ((step + 1) % 2) - 1) * (2 * pair - 1)).astype(F32)
@@ -347,14 +394,21 @@
                 @pl.when(step >= TAYLOR - 2)
                 def _():
                     back_copy((step + 1) % 2).start()
+
+                @pl.when(step == TAYLOR - 1)
+                def _():
+                    multipoles(step, pair)
         return carry
 
     lax.fori_loop(0, TAYLOR, order, 0)
 
-    back_copy(1).wait_recv()
-    back_copy(0).wait_recv()
-    out[pair] = totals[0, pair] + from_pair[1]
-    out[other] = totals[1, pair] + from_pair[0]
+    for which, component in ((0, pair), (1, other)):
+        back_copy(1 - which).wait_recv()
+        for row in range(rows):
+            here = pl.ds(row * cols, cols)
+            out[pl.ds(component * rows + row, ch, stride=stride), :] = (
+                totals[which, pair, :, here] + from_pair[1 - which, :, here]
+            )
 
     psi_copy().wait_send()
     weight_copy().wait_send()
@@ -384,25 +438,33 @@
     width = rows * cols
     nmp = coupling.shape[1]
     edge = HALO * cols
-    wave = jnp.transpose(wavefunction, (1, 0, 2, 3)).reshape(parts, ch, width)
+    wave = wavefunction.reshape(ch * parts * rows, cols)
+    message = (nmp // 2 + 2) * ch + -(-(nmp + 2) // 8) * 8
+    there = pl.BlockSpec(memory_space=pl.ANY)
     vmem = pl.BlockSpec(memory_space=pltpu.VMEM)
     smem = pl.BlockSpec(memory_space=pltpu.SMEM)
     dma = pltpu.SemaphoreType.DMA
     result = pl.pallas_call(
-        functools.partial(kernel, blocks, tiles, cols),
-        out_shape=jax.ShapeDtypeStruct((parts, ch, width), F32),
-        in_specs=[vmem, vmem, vmem, vmem, smem, smem],
+        functools.partial(kernel, blocks, tiles, rows),
+        out_shape=jax.ShapeDtypeStruct(wave.shape, F32),
+        in_specs=[there, vmem, there, there, smem, smem],
         out_specs=vmem,
         scratch_shapes=[
+            pltpu.VMEM(wave.shape, F32),
+            pltpu.VMEM((nmp, ch, ch), F32),
+            pltpu.VMEM((2, ch, ch), F32),
+            pltpu.VMEM((ch, width), F32),
             pltpu.VMEM((TAYLOR + 1, 2, ch, width + 2 * edge), F32),
             pltpu.VMEM((TAYLOR, 3, ch, width), F32),
-            pltpu.VMEM((2, nmp + 3, ch, ch), F32),
-            pltpu.VMEM((2, 2, ch, ch), F32),
+            pltpu.VMEM((2, message, ch), F32),
+            pltpu.VMEM((2, 2, ch, cols), F32),
+            pltpu.VMEM((2, 2 * ch, ch), F32),
             pltpu.VMEM((2, nmp // 2 * ch, 6 * ch), BF16),
             pltpu.VMEM((2, 2 * ch, 6 * ch), BF16),
             pltpu.VMEM((2, ch, width), F32),
             pltpu.VMEM((2, 2, ch, width), F32),
             pltpu.VMEM((2, ch, width), F32),
+            dma((3,)),
             dma((2,)),
             dma((2,)),
             dma((TAYLOR, 2, 2)),
@@ -416,8 +478,8 @@
         compiler_params=pltpu.CompilerParams(
             collective_id=0, has_side_effects=True, vmem_limit_bytes=48 * 1024 * 1024
         ),
-    )(wave, l_table, coupling[0], dipole[0], selection, field)
-    return jnp.transpose(result.reshape(parts, ch, rows, cols), (1, 0, 2, 3))
+    )(wave, l_table.T, coupling[0], dipole[0], selection, field)
+    return result.reshape(wavefunction.shape)
 
 
 def solution(mesh):

time: 85 us -> 78.2 us (0.920)
  Pallas kernels: 79.2 us -> 72.3 us
    pallas_call x1, Pallas kernels: 79.2 us -> 72.3 us  [per_device(): pl.pallas_call(functools.partial(kernel, blocks, tiles, rows), out_shape=...]
    unnamed x10 -> x11, local copies, waits for them, and re-layouts: 1.68 us -> 4.81 us
    reshape x2 -> x0, local copies, waits for them, and re-layouts: 2.08 us -> none  [per_device(): wave = jnp.transpose(wavefunction, (1, 0, 2, 3)).reshape(parts, ch, width)]
    transpose x1 -> x0, local copies, waits for them, and re-layouts: 1.05 us -> none  [per_device(): return jnp.transpose(result.reshape(parts, ch, rows, cols), (1, 0, 2, 3))]
where the time goes in v1:
time: 78.2 us; the launch traced here: 77.7 us
  Pallas kernels  72.3 us (92%)
  local copies, waits for them, and re-layouts  4.81 us (6%)
    pallas_call x1, Pallas kernels, per_device(): pl.pallas_call(functools.partial(kernel, blocks, tiles, rows), out_shape=...  72.3 us
    unnamed x11, local copies, waits for them, and re-layouts  4.81 us

profile of v1, /device:TPU:13, one launch (start us, length us, event | category | flops | bytes accessed | tf_op | source)
XLA Modules:
  0.0 77.7 jit_solution(699172647894770611)
XLA Ops:
  0.7 0.0 copy-start.3
  0.7 0.0 copy-start.4
  0.7 0.7 copy-done.3
  1.3 0.0 copy-done.4
  1.3 0.0 copy-start
  1.3 1.2 %copy-done = f32[128,2,8,128]{3,2,1,0:T(8,128)S(1)} copy-done((f32[128,2,8,128]{3,2,1,0:T(8,128)S(1)}, f32[128,2,8,128]{3,2,1,0:T(8,128)}, u32[]{:S(2)}) %copy-start) | copy-done | bytes 1048600
  2.6 0.0 copy-start.1
  2.6 1.0 %copy-done.1 = f32[1,8,128,128]{3,2,1,0:T(8,128)S(1)} copy-done((f32[1,8,128,128]{3,2,1,0:T(8,128)S(1)}, f32[1,8,128,128]{3,2,1,0:T(8,128)}, u32[]{:S(2)}) %copy-start.1) | copy-done | bytes 524312
  3.6 0.0 copy-start.2
  3.6 0.9 %copy-done.2 = f32[1,2,128,128]{3,2,1,0:T(8,128)S(1)} copy-done((f32[1,2,128,128]{3,2,1,0:T(8,128)S(1)}, f32[1,2,128,128]{3,2,1,0:T(8,128)}, u32[]{:S(2)}) %copy-start.2) | copy-done | bytes 131096
  4.5 72.3 %shard_map.64 = f32[2048,128]{1,0:T(8,128)S(1)} custom-call(f32[2048,128]{1,0:T(8,128)S(1)} %bitcast.6, s32[2,128]{1,0:T(2,128)S(1)} %bitcast.9, f32[8,128,128]{2,1,0:T(8,128)S(1)} %bitcast.7, f32[2,128,128]{2,1,0:T(8,128)S(1)} %bitcast.8, s32[1,8]{1,0:T(1,128)S(1)} %copy-done.4, f32[1]{0:T(128)S(6)} %copy.8.field), custom_call_target="tpu_custom_call" | custom-call | tf_op jit(solution)/shard_map/pallas_call | solution.py:447
  76.8 1.0 %copy.9 = f32[128,2,8,128]{3,2,1,0:T(8,128)} copy(f32[128,2,8,128]{3,2,1,0:T(8,128)S(1)} %bitcast.5) | data formatting | bytes 2097152
Async XLA Ops:
  0.7 0.7 copy-start.3
  0.7 0.7 copy-start.4
  1.3 1.2 %copy-start = (f32[128,2,8,128]{3,2,1,0:T(8,128)S(1)}, f32[128,2,8,128]{3,2,1,0:T(8,128)}, u32[]{:S(2)}) copy-start(f32[128,2,8,128]{3,2,1,0:T(8,128)} %param.6) | copy-start | bytes 3145732
  2.6 1.0 %copy-start.1 = (f32[1,8,128,128]{3,2,1,0:T(8,128)S(1)}, f32[1,8,128,128]{3,2,1,0:T(8,128)}, u32[]{:S(2)}) copy-start(f32[1,8,128,128]{3,2,1,0:T(8,128)} %param.8) | copy-start | bytes 1572868
  3.6 0.9 %copy-start.2 = (f32[1,2,128,128]{3,2,1,0:T(8,128)S(1)}, f32[1,2,128,128]{3,2,1,0:T(8,128)}, u32[]{:S(2)}) copy-start(f32[1,2,128,128]{3,2,1,0:T(8,128)} %param.10) | copy-start | bytes 393220

commit v2 on v1

--- a/solution.py
+++ b/solution.py
@@ -30,10 +30,10 @@
 
 
 def kernel(
-    blocks, tiles, rows, wave_in, angular, coupling_in, dipole_in, selection, field, out,
-    wave, coupling, dipole, start_other,
+    blocks, tiles, rows, wave_in, angular_in, coupling_in, dipole_in, selection, field, out,
+    wave, angular, coupling, dipole, start_other,
     state, near, weights, central, lower, w_stack, d_stack, part, totals, from_pair,
-    load_sem, psi_sem, wgt_sem, core_sem, z_sem, down_sem, up_sem, dcore_sem, dz_sem, back_sem,
+    load_sem, psi_sem, wgt_sem, relay_sem, core_sem, z_sem, down_sem, up_sem, dcore_sem, dz_sem, back_sem,
 ):
     ch = coupling.shape[1]
     nmp = coupling.shape[0]
@@ -44,6 +44,8 @@
     side = (quad + 2) * ch
     edge = HALO * cols
     mid = pl.ds(edge, width)
+    span = ROWS * cols
+    chunks = rows // ROWS
 
     me = lax.axis_index("lblk")
     tile = lax.axis_index("tile")
@@ -55,6 +57,7 @@
     to_pair = {"lblk": me + 2 - 4 * pair}
     to_core = {"lblk": me + 1 - 2 * core}
     to_z = {"lblk": me + 6 * core - 3}
+    to_relay = {"tile": tile + 1 - 2 * (tile % 2)}
     to_low = {"tile": tile - 1}
     to_high = {"tile": tile + 1}
     has_z = jnp.logical_or(
@@ -69,17 +72,33 @@
             device_id=target, device_id_type=MESH,
         )
 
-    def psi_copy():
-        return remote(start_other, state.at[0, pair, :, mid], psi_sem, to_pair)
+    def chunk_at(at, offset=0):
+        return pl.ds(pl.multiple_of(offset + at * span, cols), span)
+
+    def psi_copy(at):
+        return remote(
+            start_other.at[:, chunk_at(at)], state.at[0, pair, :, chunk_at(at, edge)],
+            psi_sem.at[at], to_pair,
+        )
+
+    relayed = tiles % 2 == 0
+    length = weights.shape[1] // 2 if relayed else weights.shape[1]
+    half = pl.ds(pl.multiple_of(tile % 2 * length, 8), length) if relayed else pl.ds(0, length)
 
     def weight_copy():
-        return remote(weights.at[pair], weights.at[pair], wgt_sem, to_pair)
+        return remote(weights.at[pair, half], weights.at[pair, half], wgt_sem, to_pair)
+
+    def relay_copy():
+        return remote(weights.at[other, half], weights.at[other, half], relay_sem, to_relay)
 
     def core_copy(step, b):
         return remote(state.at[step, b, :, mid], near.at[step, core + b], core_sem.at[step, b], to_core)
 
-    def z_copy(step):
-        return remote(state.at[step, core, :, mid], near.at[step, 2 * (1 - core)], z_sem.at[step], to_z)
+    def z_copy(step, at):
+        return remote(
+            state.at[step, core, :, chunk_at(at, edge)],
+            near.at[step, 2 * (1 - core), :, chunk_at(at)], z_sem.at[step, at], to_z,
+        )
 
     def low_copy(step, b):
         return remote(
@@ -93,25 +112,24 @@
             up_sem.at[step, b], to_high,
         )
 
-    def send_block(step, b):
+    def send_chunk(step, b, at):
         @pl.when(jnp.logical_and(b == core, has_z))
         def _():
-            z_copy(step).start()
-
-        @pl.when(has_low)
+            z_copy(step, at).start()
+
+        @pl.when(jnp.logical_and(at == 0, has_low))
         def _():
             low_copy(step, b).start()
 
-        @pl.when(has_high)
+        @pl.when(jnp.logical_and(at == chunks - 1, has_high))
         def _():
             high_copy(step, b).start()
-
-        core_copy(step, b).start()
 
     def wait_sent(step, b):
         @pl.when(jnp.logical_and(b == core, has_z))
         def _():
-            z_copy(step).wait_send()
+            for at in range(chunks):
+                z_copy(step, at).wait_send()
 
         @pl.when(has_low)
         def _():
@@ -132,8 +150,11 @@
         def _():
             high_copy(step, b).wait_recv()
 
-    def back_copy(which):
-        return remote(totals.at[which, other], from_pair.at[which], back_sem.at[which], to_pair)
+    def back_copy(which, at):
+        return remote(
+            totals.at[which, other, :, chunk_at(at)], from_pair.at[which, :, chunk_at(at)],
+            back_sem.at[which, at], to_pair,
+        )
 
     def dcore_low(b):
         return remote(weights.at[b, pl.ds(quad * ch, 2 * ch)], lower.at[b], dcore_sem.at[b], to_core)
@@ -146,7 +167,7 @@
 
     loads = [
         pltpu.make_async_copy(src, dst, load_sem.at[at])
-        for at, (src, dst) in enumerate(((wave_in, wave), (coupling_in, coupling), (dipole_in, dipole)))
+        for at, (src, dst) in enumerate(((wave_in, wave), (coupling_in, coupling), (dipole_in, dipole), (angular_in, angular)))
     ]
     for load in loads:
         load.start()
@@ -173,8 +194,10 @@
         peers = peers + there.astype(jnp.int32)
     pl.semaphore_wait(barrier, peers)
 
-    psi_copy().start()
-    send_block(0, pair)
+    psi_copy(0).start()
+    for at in range(chunks):
+        send_chunk(0, pair, at)
+    core_copy(0, pair).start()
 
     def put_weight(b, k, matrix):
         at = pl.ds(k % quad * ch, ch)
@@ -186,6 +209,7 @@
 
     at_row = lax.broadcasted_iota(jnp.int32, (ch, ch), 0)
     at_col = lax.broadcasted_iota(jnp.int32, (ch, ch), 1)
+    loads[3].wait()
     momenta = angular[...].astype(F32)
     momenta = 0.5 * momenta * (momenta + 1.0)
     weights[pair, pl.ds(side, 2)] = momenta
@@ -205,6 +229,8 @@
     for a in range(2):
         weights[pair, pl.ds((quad + a) * ch, ch)] = dipole[a]
     weight_copy().start()
+    for at in range(1, chunks):
+        psi_copy(at).start()
 
     def unpack(b):
         for k in range(quad):
@@ -245,8 +271,6 @@
                 d_stack[b, at, pl.ds(part_at * ch, ch)] = high
                 d_stack[b, at, pl.ds((2 + part_at) * ch, ch)] = low
                 d_stack[b, at, pl.ds((4 + part_at) * ch, ch)] = high
-
-    span = ROWS * cols
 
     def radii(at):
         index = lax.broadcasted_iota(jnp.int32, (1, span), 1)
@@ -279,6 +303,10 @@
         lane_at = lax.broadcasted_iota(jnp.int32, (1, cols), 1)
 
         def body(at, carry):
+            @pl.when(jnp.logical_and(b == core, has_z))
+            def _():
+                z_copy(step, at).wait_recv()
+
             one, two = radii(at)
             here = pl.ds(pl.multiple_of(at * span, cols), span)
             up = near[step, b + 1, :, here]
@@ -318,34 +346,54 @@
             state[step + 1, b, :, pl.ds(start, span)] = term
             which = (step + 1) % 2
             totals[which, b, :, here] = totals[which, b, :, here] + term
+
+            @pl.when(step < TAYLOR - 1)
+            def _():
+                send_chunk(step + 1, b, at)
+
+            @pl.when(jnp.logical_and(step >= TAYLOR - 2, b == other))
+            def _():
+                back_copy(which, at).start()
             return carry
 
         lax.fori_loop(0, rows // ROWS, body, 0)
 
     spread(pair)
     multipoles(0, pair)
-    psi_copy().wait_recv()
-    send_block(0, other)
+    weight_copy().wait_recv()
+    if relayed:
+        relay_copy().start()
+
+    def pass_on(at):
+        psi_copy(at).wait_recv()
+        send_chunk(0, other, at)
+
+    for at in range(chunks // 2):
+        pass_on(at)
+    if relayed:
+        relay_copy().wait_recv()
+
+    @pl.when(core == 0)
+    def _():
+        dcore_low(0).start()
+        dcore_low(1).start()
+
+    @pl.when(core == 1)
+    def _():
+        dcore_high().start()
+
+        @pl.when(has_z)
+        def _():
+            dz_copy().start()
+
+    unpack(other)
+    spread(other)
+    for at in range(chunks // 2, chunks):
+        pass_on(at)
+    core_copy(0, other).start()
     for b in range(2):
         totals[0, b] = state[0, b, :, mid]
         totals[1, b] = jnp.zeros((ch, width), F32)
-    weight_copy().wait_recv()
-
-    @pl.when(core == 0)
-    def _():
-        dcore_low(0).start()
-        dcore_low(1).start()
-
-    @pl.when(core == 1)
-    def _():
-        dcore_high().start()
-
-        @pl.when(has_z)
-        def _():
-            dz_copy().start()
-
-    unpack(other)
-    spread(other)
     multipoles(0, other)
 
     @pl.when(core == 1)
@@ -365,52 +413,53 @@
     stack_dipoles(1)
 
     def order(step, carry):
+        last = step == TAYLOR - 1
+        first = jnp.where(last, other, core)
+        second = 1 - first
+
         @pl.when(step > 0)
         def _():
-            multipoles(step, other)
+            multipoles(step, first)
 
         @pl.when(jnp.logical_and(step > 0, step < TAYLOR - 1))
         def _():
-            multipoles(step, pair)
+            multipoles(step, second)
 
         sign = ((2 * ((step + 1) % 2) - 1) * (2 * pair - 1)).astype(F32)
         scale = sign * (time_step / (step + 1).astype(F32))
         core_copy(step, 0).wait_recv()
         core_copy(step, 1).wait_recv()
-
-        @pl.when(has_z)
-        def _():
-            z_copy(step).wait_recv()
-
-        for b in (other, pair):
+        for b in (first, second):
             wait_halo(step, b)
             finish(step, b, scale)
 
             @pl.when(step < TAYLOR - 1)
             def _():
-                send_block(step + 1, b)
-
-            if b is other:
-                @pl.when(step >= TAYLOR - 2)
+                core_copy(step + 1, b).start()
+
+            if b is first:
+                @pl.when(last)
                 def _():
-                    back_copy((step + 1) % 2).start()
-
-                @pl.when(step == TAYLOR - 1)
-                def _():
-                    multipoles(step, pair)
+                    multipoles(step, second)
         return carry
 
     lax.fori_loop(0, TAYLOR, order, 0)
 
     for which, component in ((0, pair), (1, other)):
-        back_copy(1 - which).wait_recv()
-        for row in range(rows):
-            here = pl.ds(row * cols, cols)
-            out[pl.ds(component * rows + row, ch, stride=stride), :] = (
-                totals[which, pair, :, here] + from_pair[1 - which, :, here]
-            )
-
-    psi_copy().wait_send()
+        for at in range(chunks):
+            back_copy(1 - which, at).wait_recv()
+            for row in range(at * ROWS, (at + 1) * ROWS):
+                here = pl.ds(row * cols, cols)
+                out[pl.ds(component * rows + row, ch, stride=stride), :] = (
+                    totals[which, pair, :, here] + from_pair[1 - which, :, here]
+                )
+
+    for at in range(chunks):
+        psi_copy(at).wait_send()
+        back_copy(0, at).wait_send()
+        back_copy(1, at).wait_send()
+    if relayed:
+        relay_copy().wait_send()
     weight_copy().wait_send()
     for step in range(TAYLOR):
         for b in range(2):
@@ -428,9 +477,6 @@
         @pl.when(has_z)
         def _():
             dz_copy().wait_send()
-
-    back_copy(0).wait_send()
-    back_copy(1).wait_send()
 
 
 def per_device(blocks, tiles, wavefunction, l_table, coupling, selection, dipole, field):
@@ -440,17 +486,19 @@
     edge = HALO * cols
     wave = wavefunction.reshape(ch * parts * rows, cols)
     message = (nmp // 2 + 2) * ch + -(-(nmp + 2) // 8) * 8
-    there = pl.BlockSpec(memory_space=pl.ANY)
+    there = pl.BlockSpec(memory_space=pltpu.HBM)
+    chunks = rows // ROWS
     vmem = pl.BlockSpec(memory_space=pltpu.VMEM)
     smem = pl.BlockSpec(memory_space=pltpu.SMEM)
     dma = pltpu.SemaphoreType.DMA
     result = pl.pallas_call(
         functools.partial(kernel, blocks, tiles, rows),
         out_shape=jax.ShapeDtypeStruct(wave.shape, F32),
-        in_specs=[there, vmem, there, there, smem, smem],
+        in_specs=[there, there, there, there, smem, smem],
         out_specs=vmem,
         scratch_shapes=[
             pltpu.VMEM(wave.shape, F32),
+            pltpu.VMEM((2, ch), jnp.int32),
             pltpu.VMEM((nmp, ch, ch), F32),
             pltpu.VMEM((2, ch, ch), F32),
             pltpu.VMEM((ch, width), F32),
@@ -464,19 +512,20 @@
             pltpu.VMEM((2, ch, width), F32),
             pltpu.VMEM((2, 2, ch, width), F32),
             pltpu.VMEM((2, ch, width), F32),
-            dma((3,)),
+            dma((4,)),
+            dma((chunks, 2)),
             dma((2,)),
             dma((2,)),
             dma((TAYLOR, 2, 2)),
-            dma((TAYLOR, 2)),
+            dma((TAYLOR, chunks, 2)),
             dma((TAYLOR, 2, 2)),
             dma((TAYLOR, 2, 2)),
             dma((2, 2)),
             dma((2,)),
-            dma((2, 2)),
+            dma((2, chunks, 2)),
         ],
         compiler_params=pltpu.CompilerParams(
-            collective_id=0, has_side_effects=True, vmem_limit_bytes=48 * 1024 * 1024
+            collective_id=0, has_side_effects=True, vmem_limit_bytes=63 * 1024 * 1024
         ),
     )(wave, l_table.T, coupling[0], dipole[0], selection, field)
     return result.reshape(wavefunction.shape)

time: 78.2 us -> 67.5 us (0.86)
  Pallas kernels: 72.3 us -> 63.7 us
  local copies, waits for them, and re-layouts: 4.81 us -> 2.26 us
    pallas_call x1, Pallas kernels: 72.3 us -> 63.7 us  [per_device(): pl.pallas_call(functools.partial(kernel, blocks, tiles, rows), out_shape=...]
    unnamed x11 -> x1, local copies, waits for them, and re-layouts: 4.81 us -> 2.26 us
where the time goes in v2:
time: 67.5 us; the launch traced here: 66.6 us
  Pallas kernels  63.7 us (94%)
  local copies, waits for them, and re-layouts  2.26 us (3%)
    pallas_call x1, Pallas kernels, per_device(): pl.pallas_call(functools.partial(kernel, blocks, tiles, rows), out_shape=...  63.7 us
    unnamed x1, local copies, waits for them, and re-layouts  2.26 us

profile of v2, /device:TPU:13, one launch (start us, length us, event | category | flops | bytes accessed | tf_op | source)
XLA Modules:
  0.0 66.6 jit_solution(13918261345989956329)
XLA Ops:
  0.7 63.7 %shard_map.64 = f32[2048,128]{1,0:T(8,128)} custom-call(f32[2048,128]{1,0:T(8,128)} %bitcast.6, s32[2,128]{1,0:T(2,128)} %bitcast.9, f32[8,128,128]{2,1,0:T(8,128)} %bitcast.7, f32[2,128,128]{2,1,0:T(8,128)} %bitcast.8, s32[1,8]{1,0:T(1,128)} %selection.1, f32[1]{0:T(128)S(6)} %copy.8.field), custom_call_target="tpu_custom_call" | custom-call | tf_op jit(solution)/shard_map/pallas_call | solution.py:494
  64.4 2.3 %copy.9 = f32[128,2,8,128]{3,2,1,0:T(8,128)} copy(f32[128,2,8,128]{3,2,1,0:T(8,128)} %bitcast.5) | data formatting | bytes 2097152

commit v3 on v2

--- a/solution.py
+++ b/solution.py
@@ -30,10 +30,10 @@
 
 
 def kernel(
-    blocks, tiles, rows, wave_in, angular_in, coupling_in, dipole_in, selection, field, out,
-    wave, angular, coupling, dipole, start_other,
+    blocks, tiles, rows, wave_in, angular_in, coupling_in, dipole_in, selection, field, mine_out, theirs_out,
+    mine, theirs, wave, angular, coupling, dipole, start_other,
     state, near, weights, central, lower, w_stack, d_stack, part, totals, from_pair,
-    load_sem, psi_sem, wgt_sem, relay_sem, core_sem, z_sem, down_sem, up_sem, dcore_sem, dz_sem, back_sem,
+    load_sem, store_sem, psi_sem, wgt_sem, relay_sem, core_sem, z_sem, down_sem, up_sem, dcore_sem, dz_sem, back_sem,
 ):
     ch = coupling.shape[1]
     nmp = coupling.shape[0]
@@ -296,7 +296,7 @@
             part[b, :, pl.ds(pl.multiple_of(at * span, cols), span)] = result * inverse
             return carry
 
-        lax.fori_loop(0, rows // ROWS, body, 0)
+        lax.fori_loop(0, rows // ROWS, body, 0, unroll=True)
 
     def finish(step, b, scale):
         strength = field[0]
@@ -356,7 +356,7 @@
                 back_copy(which, at).start()
             return carry
 
-        lax.fori_loop(0, rows // ROWS, body, 0)
+        lax.fori_loop(0, rows // ROWS, body, 0, unroll=True)
 
     spread(pair)
     multipoles(0, pair)
@@ -445,14 +445,25 @@
 
     lax.fori_loop(0, TAYLOR, order, 0)
 
+    def rows_of(component, row):
+        return pl.ds(component * rows + row, ch, stride=stride)
+
     for which, component in ((0, pair), (1, other)):
+        for row in range(rows):
+            mine[rows_of(component, row), :] = totals[which, pair, :, pl.ds(row * cols, cols)]
+    stores = [
+        pltpu.make_async_copy(src, dst, store_sem.at[at])
+        for at, (src, dst) in enumerate(((mine, mine_out), (theirs, theirs_out)))
+    ]
+    stores[0].start()
+    for which, component in ((1, pair), (0, other)):
         for at in range(chunks):
-            back_copy(1 - which, at).wait_recv()
+            back_copy(which, at).wait_recv()
             for row in range(at * ROWS, (at + 1) * ROWS):
-                here = pl.ds(row * cols, cols)
-                out[pl.ds(component * rows + row, ch, stride=stride), :] = (
-                    totals[which, pair, :, here] + from_pair[1 - which, :, here]
-                )
+                theirs[rows_of(component, row), :] = from_pair[which, :, pl.ds(row * cols, cols)]
+    stores[1].start()
+    for store in stores:
+        store.wait()
 
     for at in range(chunks):
         psi_copy(at).wait_send()
@@ -488,15 +499,16 @@
     message = (nmp // 2 + 2) * ch + -(-(nmp + 2) // 8) * 8
     there = pl.BlockSpec(memory_space=pltpu.HBM)
     chunks = rows // ROWS
-    vmem = pl.BlockSpec(memory_space=pltpu.VMEM)
     smem = pl.BlockSpec(memory_space=pltpu.SMEM)
     dma = pltpu.SemaphoreType.DMA
-    result = pl.pallas_call(
+    mine, theirs = pl.pallas_call(
         functools.partial(kernel, blocks, tiles, rows),
-        out_shape=jax.ShapeDtypeStruct(wave.shape, F32),
+        out_shape=[jax.ShapeDtypeStruct(wave.shape, F32)] * 2,
         in_specs=[there, there, there, there, smem, smem],
-        out_specs=vmem,
+        out_specs=[there, there],
         scratch_shapes=[
+            pltpu.VMEM(wave.shape, F32),
+            pltpu.VMEM(wave.shape, F32),
             pltpu.VMEM(wave.shape, F32),
             pltpu.VMEM((2, ch), jnp.int32),
             pltpu.VMEM((nmp, ch, ch), F32),
@@ -513,6 +525,7 @@
             pltpu.VMEM((2, 2, ch, width), F32),
             pltpu.VMEM((2, ch, width), F32),
             dma((4,)),
+            dma((2,)),
             dma((chunks, 2)),
             dma((2,)),
             dma((2,)),
@@ -528,7 +541,7 @@
             collective_id=0, has_side_effects=True, vmem_limit_bytes=63 * 1024 * 1024
         ),
     )(wave, l_table.T, coupling[0], dipole[0], selection, field)
-    return result.reshape(wavefunction.shape)
+    return (mine + theirs).reshape(wavefunction.shape)
 
 
 def solution(mesh):

time: 67.5 us -> 67.2 us (level)
  other arithmetic: 0 us -> 2.62 us
  local copies, waits for them, and re-layouts: 2.26 us -> 0 us
    add x0 -> x1, other arithmetic: none -> 2.62 us  [per_device(): return (mine + theirs).reshape(wavefunction.shape)]
    unnamed x1 -> x0, local copies, waits for them, and re-layouts: 2.26 us -> none
where the time goes in v3:
time: 67.2 us; the launch traced here: 67 us
  Pallas kernels  63.7 us (95%)
  other arithmetic  2.62 us (4%)
    pallas_call x1, Pallas kernels, per_device(): pl.pallas_call(functools.partial(kernel, blocks, tiles, rows), out_shape=...  63.7 us
    add x1, other arithmetic, per_device(): return (mine + theirs).reshape(wavefunction.shape)  2.62 us

profile of v3, /device:TPU:13, one launch (start us, length us, event | category | flops | bytes accessed | tf_op | source)
XLA Modules:
  0.0 67.0 jit_solution(6470102109050059156)
XLA Ops:
  0.7 63.7 %shard_map.64 = (f32[2048,128]{1,0:T(8,128)}, f32[2048,128]{1,0:T(8,128)}) custom-call(f32[2048,128]{1,0:T(8,128)} %bitcast.5, s32[2,128]{1,0:T(2,128)} %bitcast.8, f32[8,128,128]{2,1,0:T(8,128)} %bitcast.6, f32[2,128,128]{2,1,0:T(8,128)} %bitcast.7, s32[1,8]{1,0:T(1,128)} %selection.1, f32[1]{0:T(128)S(6)} %copy.7.field), custom_call_target="tpu_custom_call" | custom-call | tf_op jit(solution)/shard_map/pallas_call | solution.py:504
  64.4 2.6 %add.3 = f32[2048,128]{1,0:T(8,128)} add(f32[2048,128]{1,0:T(8,128)} %get-tuple-element.7, f32[2048,128]{1,0:T(8,128)} %get-tuple-element.8) | non-fusion elementwise | flops 262144 | bytes 3145728 | tf_op jit(solution)/shard_map/add | solution.py:544
